TPU v7x, 32 devices: a whole 2x2x4 slice. The times are simulated.
32 devices in a mesh: pole: 2 (over x), row: 8 (over z, y), col: 2 (over core).
Axes of the slice: x: 2, y: 2, z: 4, core: 2. Of those that a mesh axis runs over, the one named last changes fastest.
Arguments:
- ancestor_inverse: float32 [2, 24576, 12288], P(None, ('pole', 'row'), 'col'), parts along dimension 1, may hold values from -6 to 6
- factor_panels: float32 [4, 2, 24576, 128], P(None, None, ('pole', 'col', 'row')), parts along dimension 2, may hold values from -0.0546875 to 0.0546875
- diag_inverse: float32 [8, 2, 128, 128], P('pole'), parts along dimension 0, may hold values from -6 to 6
- coupling: float32 [4, 2, 128, 128], P('pole'), parts along dimension 0, may hold values from -0.5 to 0.5
- block_pattern: int32 [4, 96], replicated, may hold values from 0 to 1, as said below
- tree_order: int32 [4], replicated, may hold values from 0 to 3, each once
Outputs:
- inverse_panels: float32 [4, 2, 24576, 128], P(None, None, ('pole', 'row')), parts along dimension 2
- inverse_diagonal: float32 [8, 2, 128, 128], P('pole'), parts along dimension 0
- inverse_coupling: float32 [4, 2, 128, 128], P('pole'), parts along dimension 0
There are 2 independent parts, one for each index of `pole`. A program takes and returns all parts, laid end to end along the dimension named above; an argument that names none is the same for every part. Nothing has to cross between parts.
Inputs may be any that keep to these rules, and one draw needn't show every extreme that they name: `tree_order`: each supernode number appears once. `block_pattern`: blocks 0 and 48 lie in every supernode's structure.
All inputs are finite; a program needn't handle non-finite values.
Results may differ from a plain program's by a relative error of at most 0.0001.
Values sent between devices are 32-bit elements; how exact they have to be, the bound alone decides.
No kernel may reach another device: no remote copies, remote signals or barrier semaphores. Data moves between devices by JAX's collectives and lax.ppermute only.
A program may use at most 192 MiB of HBM per device.

v0:
```python
import functools

import jax
import jax.numpy as jnp
from jax import lax
from jax.experimental import pallas as pl
from jax.experimental.pallas import tpu as pltpu
from jax.sharding import PartitionSpec as P


def matmul(left_side, right_side):
    return jnp.dot(
        left_side, right_side, preferred_element_type=jnp.float32, precision=lax.Precision.HIGHEST
    )


def multiply(left_side, right_side):
    real_part = matmul(left_side[0], right_side[0]) - matmul(left_side[1], right_side[1])
    imag_part = matmul(left_side[0], right_side[1]) + matmul(left_side[1], right_side[0])
    return jnp.stack([real_part, imag_part])


def flipped(matrix):
    return jnp.swapaxes(matrix, 1, 2)


def halves(value):
    high = value.astype(jnp.bfloat16)
    low = (value - high.astype(jnp.float32)).astype(jnp.bfloat16)
    return high, low


def dot32(left_side, right_side, contract=((1,), (0,))):
    return lax.dot_general(
        left_side, right_side, (contract, ((), ())), preferred_element_type=jnp.float32
    )


def dot3(left_side, right_side, contract=((1,), (0,))):
    return (
        dot32(left_side[0], right_side[0], contract)
        + dot32(left_side[0], right_side[1], contract)
        + dot32(left_side[1], right_side[0], contract)
    )


ARRIVALS = (
    ("own", False, (0, 1, 2, 3)),
    ("right 1", False, (None, 0, 1, 2)),
    ("left 1", False, (1, 2, 3, None)),
    ("over 1", True, (0, 1, 2, 3)),
    ("right 2", False, (None, None, 0, 1)),
    ("left 2", False, (2, 3, None, None)),
    ("out 2", True, (None, 0, 3, None)),
    ("over 2", True, (1, 2, 1, 2)),
    ("right 3", False, (None, None, None, 0)),
    ("left 3", False, (3, None, None, None)),
    ("over 3", True, (2, 3, 0, 1)),
    ("over 4", True, (3, None, None, 0)),
)
LINES = len(ARRIVALS[0][2])


class Layout:
    def __init__(self, rows, cols, a_shape, p_shape):
        self.rows, self.cols = rows, cols
        self.lines = rows // 2
        self.slots, _, self.piece_rows, self.block = p_shape
        self.tile_rows, self.half_rows = a_shape[1:]
        self.piece_blocks = self.piece_rows // self.block
        self.tile_blocks = self.tile_rows // self.block
        self.half_blocks = self.half_rows // self.block
        self.units = self.piece_blocks * self.slots
        self.room = self.units - self.units // 6
        self.spare = self.units - self.room
        self.buffers = len(ARRIVALS)
        self.group = next(size for size in (4, 3, 2, 1) if self.tile_blocks % size == 0)
        self.ranks = 0
        self.source = cols * rows * self.units
        self.order = self.source + self.units
        self.live = self.order + self.slots * self.tile_blocks
        self.owners = self.live + self.slots
        self.windows = self.owners + self.buffers
        self.most = self.windows + 2
        self.total = self.most + 1


def plan_kernel(layout, place, pattern, order, plan):
    row, col = place[0], place[1]
    trees = layout.slots // 2
    names = [order[slot] for slot in range(layout.slots)]

    def live(slot, block):
        value = pattern[names[slot], block]
        if slot >= trees:
            value = value * pattern[names[slot - trees], block]
        return value

    def of_owner(owner, most):
        count = jnp.int32(0)
        for piece in range(layout.piece_blocks):
            for slot in range(layout.slots):
                value = live(slot, owner * layout.piece_blocks + piece)
                at = owner * layout.units + piece * layout.slots + slot
                plan[layout.ranks + at] = jnp.where(value > 0, count, -1)
                count = count + value
        return jnp.maximum(most, count)

    plan[layout.most] = lax.fori_loop(0, layout.cols * layout.rows, of_owner, jnp.int32(0))
    for unit in range(layout.units):
        plan[layout.source + unit] = 0
    mine = (col * layout.rows + row) * layout.units
    for unit in range(layout.units):
        rank = plan[layout.ranks + mine + unit]

        @pl.when(rank >= 0)
        def _():
            plan[layout.source + rank] = unit

    for slot in range(layout.slots):
        count = jnp.int32(0)
        values = []
        for index in range(layout.tile_blocks):
            value = live(slot, row * layout.tile_blocks + index)
            values.append(value)
            count = count + value
        plan[layout.live + slot] = count
        front, back = jnp.int32(0), count
        for index, value in enumerate(values):
            at = layout.order + slot * layout.tile_blocks + jnp.where(value > 0, front, back)
            plan[at] = index
            front, back = front + value, back + 1 - value

    line, side = row // 2, row % 2
    window_line = (row * layout.tile_blocks % layout.half_blocks) // layout.piece_blocks // 2
    windows = [jnp.int32(0), jnp.int32(0)]
    for index, (_, across, origins) in enumerate(ARRIVALS):
        owner = jnp.int32(-1)
        for at, origin in enumerate(origins):
            if origin is not None:
                from_side = 1 - side if across else side
                owner = jnp.where(line == at, origin * 2 + from_side, owner)
        plan[layout.owners + index] = owner
        for which in range(2):
            hit = owner == window_line * 2 + which
            windows[which] = jnp.where(hit, index, windows[which])
    for which in range(2):
        plan[layout.windows + which] = windows[which]


def make_plan(layout, row, col, block_pattern, tree_order):
    smem = pl.BlockSpec(memory_space=pltpu.SMEM)
    return pl.pallas_call(
        functools.partial(plan_kernel, layout),
        out_shape=jax.ShapeDtypeStruct((layout.total,), jnp.int32),
        in_specs=[smem] * 3,
        out_specs=smem,
        name="make_plan",
    )(jnp.stack([row, col]).astype(jnp.int32), block_pattern, tree_order)


def compact_kernel(layout, plan, order, panels, units, spare, sems):
    block = layout.block
    copies = []
    for unit in range(layout.units):
        source = plan[layout.source + unit]
        first = pl.multiple_of(source // layout.slots * block, block)
        inside = unit < layout.room
        copy = pltpu.make_async_copy(
            panels.at[order[source % layout.slots], :, pl.ds(first, block), :],
            units.at[unit] if inside else spare.at[unit - layout.room],
            sems.at[unit],
        )
        copy.start()
        copies.append(copy)
    for copy in copies:
        copy.wait()


def compact_units(layout, plan, tree_order, panels):
    shapes = [(count, 2, layout.block, layout.block) for count in (layout.room, layout.spare)]
    return pl.pallas_call(
        functools.partial(compact_kernel, layout),
        out_shape=[jax.ShapeDtypeStruct(shape, jnp.float32) for shape in shapes],
        grid_spec=pltpu.PrefetchScalarGridSpec(
            num_scalar_prefetch=2,
            grid=(1,),
            in_specs=[pl.BlockSpec(memory_space=pltpu.HBM)],
            out_specs=[pl.BlockSpec(shape, lambda step, *_: (0, 0, 0, 0)) for shape in shapes],
            scratch_shapes=[pltpu.SemaphoreType.DMA((layout.units,))],
        ),
        compiler_params=pltpu.CompilerParams(vmem_limit_bytes=16 * 2**20),
        name="compact_units",
    )(plan, tree_order, panels)


def owner_at(layout, which, plan, step):
    if which is None:
        return step // layout.piece_blocks
    owner = plan[layout.owners + which[0]]
    for local in range(1, len(which)):
        later = step // layout.piece_blocks >= local
        owner = jnp.where(later, plan[layout.owners + which[local]], owner)
    return owner


def gemm_kernel(layout, which, parted, first_call, plan, place, *refs):
    refs = list(refs)
    in_ref = None if first_call else refs.pop(0)
    a_ref = refs.pop(0)
    *units, out_ref, total, a_parts, weights, sems = refs
    step = pl.program_id(0)
    block, rows = layout.block, layout.tile_rows
    width = 2 * block

    def each_slot(source, target, act):
        for slot in range(layout.slots):
            getattr(pltpu.make_async_copy(source.at[slot], target.at[slot], sems.at[slot]), act)()

    @pl.when(step == 0)
    def _():
        if first_call:
            total[...] = jnp.zeros_like(total)
        else:
            each_slot(in_ref, total, "start")

    owner = owner_at(layout, which, plan, step)

    @pl.loop(0, jnp.where(owner >= 0, rows // block, 0))
    def _(index):
        span = pl.ds(pl.multiple_of(index * block, block), block)
        for part in range(2):
            high, low = halves(a_ref[part, span, :])
            a_parts[span, part * block : (part + 1) * block] = high
            a_parts[span, width + part * block : width + (part + 1) * block] = low
            a_parts[span, 2 * width + part * block : 2 * width + (part + 1) * block] = high

    if not first_call:

        @pl.when(step == 0)
        def _():
            each_slot(in_ref, total, "wait")

    base = place[1] * layout.rows * layout.units + owner * layout.units
    base = base + step % layout.piece_blocks * layout.slots
    front = units[0].shape[0]

    def places(rank):
        if which is None:
            return [(rank >= layout.room, lambda: units[0].at[owner, rank - layout.room])]
        if parted:
            lower = place[0] // 2 < LINES // 2
            inside, outside = (rank >= 0) & (rank < front), (rank >= front) & (rank < layout.room)
            return [
                (inside, lambda: units[0].at[rank]),
                (outside & ~lower, lambda: units[1].at[rank - front]),
                (outside & lower, lambda: units[2].at[rank - front]),
            ]
        inside = (rank >= 0) & (rank < layout.room)
        found = []
        for local, ref in enumerate(units):
            here = inside & (step // layout.piece_blocks == local)
            found.append((here, lambda ref=ref: ref.at[rank]))
        return found

    @pl.loop(0, jnp.where(owner >= 0, layout.slots, 0))
    def _(slot):
        rank = plan[layout.ranks + base + slot]
        if which is None:
            wanted = rank >= layout.room
        else:
            wanted = (rank >= 0) & (rank < layout.room)

        for here, find in places(rank):

            @pl.when(here)
            def _():
                unit = find()
                real, imag = unit[0], unit[1]
                real_parts, imag_parts = halves(real), halves(imag)
                for third, part in enumerate((0, 0, 1)):
                    top = third * width
                    weights[top : top + block, :block] = real_parts[part]
                    weights[top : top + block, block:] = imag_parts[part]
                    weights[top + block : top + width, :block] = -imag_parts[part]
                    weights[top + block : top + width, block:] = real_parts[part]

        @pl.when(wanted & (plan[layout.live + slot] > 0))
        def _():
            total[slot] += dot32(a_parts[...], weights[...])

    @pl.when(step == pl.num_programs(0) - 1)
    def _():
        each_slot(total, out_ref, "start")
        each_slot(total, out_ref, "wait")


def gemm_units(layout, plan, place, total, ancestor_inverse, buffers, which, parted=False):
    first_call = total is None
    totals = [] if first_call else [total]
    hbm = pl.BlockSpec(memory_space=pltpu.HBM)
    block, pieces = layout.block, layout.piece_blocks
    rows, width = layout.tile_rows, 2 * layout.block

    def column(step, plan, place):
        owner = owner_at(layout, which, plan, step)
        return 0, 0, jnp.where(owner >= 0, owner * pieces + step % pieces, 0)

    shape = (layout.slots, rows, width)
    steps = (layout.rows if which is None else len(which)) * pieces
    return pl.pallas_call(
        functools.partial(gemm_kernel, layout, which, parted, first_call),
        out_shape=jax.ShapeDtypeStruct(shape, jnp.float32),
        grid_spec=pltpu.PrefetchScalarGridSpec(
            num_scalar_prefetch=2,
            grid=(steps,),
            in_specs=[hbm] * len(totals)
            + [pl.BlockSpec((2, rows, block), column)]
            + [
                pl.BlockSpec(
                    buffer.shape,
                    lambda step, plan, place, rank=buffer.ndim: (0,) * rank,
                    pipeline_mode=pl.Buffered(1),
                )
                for buffer in buffers
            ],
            out_specs=hbm,
            scratch_shapes=[
                pltpu.VMEM(shape, jnp.float32),
                pltpu.VMEM((rows, 3 * width), jnp.bfloat16),
                pltpu.VMEM((3 * width, width), jnp.bfloat16),
                pltpu.SemaphoreType.DMA((layout.slots,)),
            ],
        ),
        input_output_aliases={} if first_call else {2: 0},
        compiler_params=pltpu.CompilerParams(vmem_limit_bytes=36 * 2**20),
        cost_estimate=pl.CostEstimate(
            flops=steps * layout.slots * 3 * 2 * rows * width * width // 2,
            bytes_accessed=steps * rows * block * 8 + 8 * layout.slots * rows * width,
            transcendentals=0,
        ),
        name="gemm_units",
    )(plan, place, *totals, ancestor_inverse, *buffers)


def window_kernel(layout, plan, place, *refs):
    buffers, (spare, out, sems) = refs[: layout.buffers - 1], refs[layout.buffers - 1 :]
    row, col = place[0], place[1]
    holds = row * layout.tile_blocks // layout.half_blocks == col
    owner = row * layout.tile_blocks % layout.half_blocks // layout.piece_blocks
    beyond = plan[layout.most] > layout.room

    def fetch(which, index):
        target = out.at[which, pl.ds(0, layout.room)]
        return pltpu.make_async_copy(buffers[index], target, sems.at[which])

    def fetch_spare(which):
        target = out.at[which, pl.ds(layout.room, layout.spare)]
        return pltpu.make_async_copy(spare.at[owner + which], target, sems.at[2 + which])

    for act in ("start", "wait"):
        for which in range(2):
            for index in range(layout.buffers - 1):

                @pl.when(holds & (plan[layout.windows + which] == index))
                def _():
                    getattr(fetch(which, index), act)()

            @pl.when(holds & beyond)
            def _():
                getattr(fetch_spare(which), act)()


def find_windows(layout, plan, place, buffers, spare):
    shape = (2, layout.units, 2, layout.block, layout.block)
    return pl.pallas_call(
        functools.partial(window_kernel, layout),
        out_shape=jax.ShapeDtypeStruct(shape, jnp.float32),
        grid_spec=pltpu.PrefetchScalarGridSpec(
            num_scalar_prefetch=2,
            grid=(1,),
            in_specs=[pl.BlockSpec(memory_space=pl.ANY)] * layout.buffers,
            out_specs=pl.BlockSpec(shape, lambda step, *_: (0, 0, 0, 0, 0)),
            scratch_shapes=[pltpu.SemaphoreType.DMA((4,))],
        ),
        compiler_params=pltpu.CompilerParams(vmem_limit_bytes=16 * 2**20),
        name="find_windows",
    )(plan, place, *buffers, spare)


def contract_kernel(layout, step_blocks, plan, place, mine, near, far, sums, acc, held, sem):
    step = pl.program_id(0)
    block, slots, trees = layout.block, layout.slots, layout.slots // 2
    row, col = place[0], place[1]
    half = row * layout.tile_blocks // layout.half_blocks
    inner = row * layout.tile_blocks % layout.half_blocks
    base = half * layout.rows * layout.units + inner * slots

    @pl.when(step == 0)
    def _():
        acc[...] = jnp.zeros_like(acc)
        for source, here in ((near, half == col), (far, half != col)):

            @pl.when(here)
            def _():
                copy = pltpu.make_async_copy(source, held, sem)
                copy.start()
                copy.wait()

    def window(slot):
        parts = []
        for at in range(step_blocks):
            index = step * step_blocks + at
            rank = plan[layout.ranks + base + index * slots + slot]
            unit = held.at[index // layout.piece_blocks, jnp.maximum(rank, 0)]
            whole = jnp.concatenate([unit[0], unit[1]], axis=1)
            parts.append(jnp.where(rank >= 0, -whole, 0.0))
        return halves(jnp.concatenate(parts, axis=0))

    rows_first = ((0,), (0,))

    @pl.loop(0, trees)
    def _(tree):
        child = tree + trees
        parent_parts = halves(mine[tree])
        child_panel = window(child)
        acc[3 * tree] += dot3(window(tree), parent_parts, rows_first)
        acc[3 * tree + 1] += dot3(child_panel, parent_parts, rows_first)
        acc[3 * tree + 2] += dot3(child_panel, halves(mine[child]), rows_first)

    @pl.when(step == pl.num_programs(0) - 1)
    def _():
        for index in range(3 * trees):
            value = acc[index]
            sums[index, 0] = value[:block, :block] - value[block:, block:]
            sums[index, 1] = value[:block, block:] + value[block:, :block]


def contract_windows(layout, plan, place, mine, near, far):
    block, slots = layout.block, layout.slots
    rows, width = layout.tile_rows, 2 * layout.block
    step_blocks = layout.group
    step_rows = step_blocks * block
    sums_shape = (3 * slots // 2, 2, block, block)
    return pl.pallas_call(
        functools.partial(contract_kernel, layout, step_blocks),
        out_shape=jax.ShapeDtypeStruct(sums_shape, jnp.float32),
        grid_spec=pltpu.PrefetchScalarGridSpec(
            num_scalar_prefetch=2,
            grid=(rows // step_rows,),
            in_specs=[pl.BlockSpec((slots, step_rows, width), lambda step, *_: (0, step, 0))]
            + [pl.BlockSpec(memory_space=pl.ANY)] * 2,
            out_specs=pl.BlockSpec(sums_shape, lambda step, *_: (0, 0, 0, 0)),
            scratch_shapes=[
                pltpu.VMEM((3 * slots // 2, width, width), jnp.float32),
                pltpu.VMEM(near.shape, jnp.float32),
                pltpu.SemaphoreType.DMA,
            ],
        ),
        compiler_params=pltpu.CompilerParams(vmem_limit_bytes=24 * 2**20),
        name="contract_windows",
    )(plan, place, mine, near, far)


def column_kernel(layout, step_blocks, first_step, plan, order, mine, other, coupling, *refs):
    step = pl.program_id(0) + first_step
    block, trees = layout.block, layout.slots // 2
    columns = refs[-1]

    def masked(slot, value):
        parts = []
        for at in range(step_blocks):
            alive = is_live(slot, step * step_blocks + at)
            parts.append(jnp.where(alive, -value[at * block : (at + 1) * block], 0.0))
        return jnp.concatenate(parts, axis=0)

    def is_live(slot, index):
        alive = jnp.bool_(False)
        for at in range(layout.tile_blocks):
            found = plan[layout.order + slot * layout.tile_blocks + at] == index
            alive = alive | (found & (at < plan[layout.live + slot]))
        return alive

    def put(slot, value):
        columns[order[slot], 0] = value[:, :block]
        columns[order[slot], 1] = value[:, block:]

    @pl.loop(0, trees)
    def _(tree):
        child = tree + trees
        real, imag = coupling[tree, 0], coupling[tree, 1]
        link = jnp.concatenate(
            [jnp.concatenate([real, imag], axis=1), jnp.concatenate([-imag, real], axis=1)], axis=0
        )
        parent_col = masked(tree, mine[tree] + other[tree])
        put(tree, parent_col)
        linked = dot3(halves(parent_col), halves(link))
        put(child, masked(child, mine[child] + other[child] + linked))


def finish_columns(layout, plan, tree_order, mine, other, coupling, begun=None):
    block, slots = layout.block, layout.slots
    rows, width = layout.tile_rows, 2 * layout.block
    step_blocks = 2 if layout.tile_blocks % 2 == 0 else 1
    step_rows = step_blocks * block
    steps = rows // step_rows
    first_step = 0 if begun is None else steps // 2
    count = steps // 2 if begun is None else steps - steps // 2
    half = pl.BlockSpec((slots, step_rows, width), lambda step, *_: (0, step + first_step, 0))
    return pl.pallas_call(
        functools.partial(column_kernel, layout, step_blocks, first_step),
        out_shape=jax.ShapeDtypeStruct((slots, 2, rows, block), jnp.float32),
        grid_spec=pltpu.PrefetchScalarGridSpec(
            num_scalar_prefetch=2,
            grid=(count,),
            in_specs=[half, half, pl.BlockSpec(coupling.shape, lambda step, *_: (0, 0, 0, 0))]
            + ([] if begun is None else [pl.BlockSpec(memory_space=pl.ANY)]),
            out_specs=pl.BlockSpec(
                (slots, 2, step_rows, block), lambda step, *_: (0, 0, step + first_step, 0)
            ),
        ),
        input_output_aliases={} if begun is None else {5: 0},
        compiler_params=pltpu.CompilerParams(vmem_limit_bytes=16 * 2**20),
        cost_estimate=pl.CostEstimate(
            flops=slots * 3 * rows * width * width // 2,
            bytes_accessed=6 * slots * rows * width,
            transcendentals=0,
        ),
        name="finish_columns",
    )(plan, tree_order, mine, other, coupling, *([] if begun is None else [begun]))


def complex_dot(left_side, right_side, contract=((1,), (0,))):
    def dot(left_part, right_part):
        return dot3(halves(left_side[left_part]), halves(right_side[right_part]), contract)

    return dot(0, 0) - dot(1, 1), dot(0, 1) + dot(1, 0)


def diagonal_kernel(order, sums, diag_in, coupling, diag_out, cross_out):
    trees = coupling.shape[0]
    for tree in range(trees):
        parent, child = order[tree], order[tree + trees]
        link = (coupling[tree, 0], coupling[tree, 1])
        parent_diag = tuple(diag_in[parent, part] - sums[3 * tree, part] for part in range(2))
        moved = complex_dot(parent_diag, link)
        between = tuple(sums[3 * tree + 1, part] for part in range(2))
        linked = complex_dot(between, link)
        cross = tuple(-(between[part].T + moved[part]) for part in range(2))
        back = complex_dot(link, cross, ((0,), (0,)))
        for part in range(2):
            diag_out[parent, part] = parent_diag[part]
            cross_out[tree, part] = cross[part]
            child_sum = sums[3 * tree + 2, part] - linked[part]
            diag_out[child, part] = diag_in[child, part] - child_sum - back[part]


def finish_diagonals(order, sums, diag_inverse, coupling):
    vmem = pl.BlockSpec(memory_space=pltpu.VMEM)
    return pl.pallas_call(
        diagonal_kernel,
        out_shape=(
            jax.ShapeDtypeStruct(diag_inverse.shape, jnp.float32),
            jax.ShapeDtypeStruct(coupling.shape, jnp.float32),
        ),
        in_specs=[pl.BlockSpec(memory_space=pltpu.SMEM), vmem, vmem, vmem],
        out_specs=(vmem, vmem),
        name="finish_diagonals",
    )(order, sums, diag_inverse, coupling)


def along(value, lines, step):
    route = [(2 * at + side, 2 * (at + step) + side) for at in lines for side in range(2)]
    return lax.ppermute(value, "row", route)


def swap(value, axis):
    return lax.ppermute(value, axis, [(at, at ^ 1) for at in range(lax.axis_size(axis))])


def pick(values, index):
    return lax.dynamic_index_in_dim(values, index, 0, keepdims=False)


def sum_devices(layout, sums, row, col, begin, end):
    lines, line, side = layout.lines, row // 2, row % 2
    parts = sums.reshape(2, 2, lines, -1, layout.block)
    mine = pick(parts, col) + swap(pick(parts, 1 - col), "col")
    came, beside = lax.optimization_barrier((swap(pick(mine, 1 - side), "row"), begin()))
    mine = pick(mine, side) + came

    def turn(value, by):
        route = [
            (2 * at + side, 2 * ((at + by) % lines) + side)
            for at in range(lines)
            for side in range(2)
        ]
        return lax.ppermute(value, "row", route)

    came = [turn(pick(mine, (line + by) % lines), by) for by in range(1, lines)]
    came, beside = lax.optimization_barrier((came, end(beside)))
    share = sum(came, pick(mine, line))
    others = [share] + [turn(share, by) for by in range(1, lines)]
    stacked = jnp.stack(others)
    whole = jnp.zeros_like(stacked)
    for by in range(lines):
        whole = lax.dynamic_update_index_in_dim(whole, others[by], (line - by) % lines, 0)
    far = swap(whole, "row")
    sides = jnp.stack([jnp.where(side == 0, whole, far), jnp.where(side == 0, far, whole)])
    opposite = swap(sides, "col")
    trees = jnp.stack([jnp.where(col == 0, sides, opposite), jnp.where(col == 0, opposite, sides)])
    return trees.reshape(sums.shape), beside


def live_units(ancestor_inverse, factor_panels, diag_inverse, coupling, block_pattern, tree_order):
    layout = Layout(
        lax.axis_size("row"), lax.axis_size("col"), ancestor_inverse.shape, factor_panels.shape
    )
    row, col = lax.axis_index("row"), lax.axis_index("col")
    place = jnp.stack([row, col]).astype(jnp.int32)
    line = row // 2
    plan = make_plan(layout, row, col, block_pattern, tree_order)
    room = layout.room
    own, spare = compact_units(layout, plan, tree_order, factor_panels)
    half = room // 2

    def multiplied(total, buffers, first):
        which = None if first is None else list(range(first, first + len(buffers)))
        return gemm_units(layout, plan, place, total, ancestor_inverse, buffers, which)

    def phase(came, total, buffers, first):
        return lax.optimization_barrier((came, multiplied(total, buffers, first)))

    def inward(values):
        return jnp.where(line < LINES // 2, values[1], values[0])

    came = along(own, range(LINES - 1), 1), along(own, range(1, LINES), -1), swap(own, "row")
    first, total = phase(came, None, [own], 0)

    def beyond(_, state):
        gathered = lax.all_gather(spare, "row", axis=0, tiled=False)
        return gathered, multiplied(state[1], [gathered], None)

    trips = (plan[layout.most] > room).astype(jnp.int32)
    spares = jnp.zeros((layout.rows,) + spare.shape, jnp.float32)
    spares, total = lax.fori_loop(0, trips, beyond, (spares, total))

    end = LINES - 1
    came = along(first[0], range(1, end), 1), along(first[1], range(1, end), -1)
    outward = [(at, at + 2) for at in range(2)] + [(at + 2 * end, at + 2 * end - 2) for at in range(2)]
    came += lax.ppermute(first[2], "row", outward), swap(inward(first), "row")
    second, total = phase(came, total, list(first), 1)
    came = along(second[0], [end - 1], 1), along(second[1], [1], -1), swap(inward(second), "row")
    third, total = phase(came, total, list(second), 4)
    rest = lax.slice_in_dim(third[2], room - half, room, axis=0)
    over = lax.slice_in_dim(inward(third), 0, room - half, axis=0)
    came = along(rest, [end - 1], 1), along(rest, [1], -1), swap(over, "row")
    total = multiplied(total, list(third), 8)
    third, total = lax.optimization_barrier((third, total))
    near = find_windows(layout, plan, place, [own, *first, *second, *third], spares)
    far = swap(near, "col")
    last, total, near = lax.optimization_barrier((came, total, near))
    last = [last[2], last[0], last[1]]
    total = gemm_units(layout, plan, place, total, ancestor_inverse, last, [11], parted=True)

    other = swap(total, "col")
    sums = contract_windows(layout, plan, place, total, near, far)
    other, sums = lax.optimization_barrier((other, sums))
    columns = functools.partial(finish_columns, layout, plan, tree_order, total, other, coupling)
    sums, inverse_panels = sum_devices(layout, sums, row, col, columns, columns)
    inverse_diagonal, inverse_coupling = finish_diagonals(tree_order, sums, diag_inverse, coupling)
    return inverse_panels, inverse_diagonal, inverse_coupling


def swapped(block, axis, bit):
    count = lax.axis_size(axis)
    route = []
    for low in range(count):
        high = low | 1 << bit
        if high != low and high < count:
            route += [(low, high), (high, low)]
    return lax.ppermute(block, axis, route)


def row_masks(pattern_eff, first_row, row_count, block_rows):
    row_index = first_row + jnp.arange(row_count, dtype=jnp.int32)
    blocks = row_index // block_rows
    onehot = (blocks[:, None] == jnp.arange(pattern_eff.shape[1], dtype=jnp.int32)[None, :]).astype(
        jnp.float32
    )
    return matmul(pattern_eff, onehot.T)


def whole_panels(ancestor_inverse, factor_panels, diag_inverse, coupling, block_pattern, tree_order):
    grid_row = lax.axis_index("row")
    grid_col = lax.axis_index("col")
    tile_rows = ancestor_inverse.shape[1]
    half_rows = ancestor_inverse.shape[2]
    piece_rows = factor_panels.shape[2]
    block_rows = factor_panels.shape[3]
    super_count = factor_panels.shape[0]
    share_rows = tile_rows // 2
    sorted_pattern = jnp.take(block_pattern, tree_order, axis=0).astype(jnp.float32)
    pattern_eff = jnp.concatenate(
        [sorted_pattern[:2], sorted_pattern[2:] * sorted_pattern[:2]], axis=0
    )
    source_mask = row_masks(
        pattern_eff, grid_col * half_rows + grid_row * piece_rows, piece_rows, block_rows
    )
    target_mask = row_masks(pattern_eff, grid_row * tile_rows, tile_rows, block_rows)
    panels = jnp.take(factor_panels, tree_order, axis=0) * source_mask[:, None, :, None]
    diag_blocks = jnp.take(diag_inverse, tree_order, axis=0)
    columns = []
    products = []
    for tree_slot in range(super_count):
        gathered = lax.all_gather(panels[tree_slot], "row", axis=1, tiled=True)
        columns.append(gathered)
        products.append(lax.psum(multiply(ancestor_inverse, gathered), "col"))
    own_flag = (grid_row * tile_rows // half_rows == grid_col).astype(jnp.float32)
    offset = jnp.clip(grid_row * tile_rows - grid_col * half_rows, 0, half_rows - tile_rows)
    own_windows = jnp.stack(
        [
            lax.dynamic_slice_in_dim(column_set, offset, tile_rows, 1) * own_flag
            for column_set in columns
        ]
    )
    partner_windows = swapped(own_windows, "col", 0)
    tile_windows = own_windows + partner_windows

    def share(matrix):
        return lax.dynamic_slice_in_dim(matrix, grid_col * share_rows, share_rows, 1)

    windows = [share(tile_windows[tree_slot]) for tree_slot in range(super_count)]
    parent_cols = [
        -target_mask[tree_slot][None, :, None] * products[tree_slot] for tree_slot in range(2)
    ]
    child_cols = [
        -target_mask[tree_slot + 2][None, :, None]
        * (products[tree_slot + 2] + multiply(parent_cols[tree_slot], coupling[tree_slot]))
        for tree_slot in range(2)
    ]
    parent_local = [
        multiply(flipped(windows[tree_slot]), share(parent_cols[tree_slot]))
        for tree_slot in range(2)
    ]
    cross_local = [
        multiply(flipped(share(parent_cols[tree_slot])), windows[tree_slot + 2])
        for tree_slot in range(2)
    ]
    child_local = [
        multiply(flipped(windows[tree_slot + 2]), share(child_cols[tree_slot]))
        for tree_slot in range(2)
    ]
    parent_sums = lax.psum(jnp.stack(parent_local), ("row", "col"))
    parent_diag = [diag_blocks[tree_slot] - parent_sums[tree_slot] for tree_slot in range(2)]
    child_totals = lax.psum(jnp.stack(cross_local + child_local), ("row", "col"))
    crosses = [
        -(child_totals[tree_slot] + multiply(parent_diag[tree_slot], coupling[tree_slot]))
        for tree_slot in range(2)
    ]
    child_sums = [child_totals[2 + tree_slot] for tree_slot in range(2)]
    child_diag = [
        diag_blocks[tree_slot + 2]
        - child_sums[tree_slot]
        - multiply(flipped(coupling[tree_slot]), crosses[tree_slot])
        for tree_slot in range(2)
    ]
    all_cols = jnp.stack(parent_cols + child_cols)
    all_diag = jnp.stack(parent_diag + child_diag)
    inverse_panels = jnp.zeros_like(all_cols).at[tree_order].set(all_cols)
    inverse_diagonal = jnp.zeros_like(all_diag).at[tree_order].set(all_diag)
    return (inverse_panels, inverse_diagonal, jnp.stack(crosses))


def per_device(ancestor_inverse, factor_panels, *others):
    row_count, col_count = lax.axis_size("row"), lax.axis_size("col")
    piece_rows, block = factor_panels.shape[2:]
    tile_rows, half_rows = ancestor_inverse.shape[1:]
    whole_blocks = piece_rows % block == 0 and half_rows % tile_rows == 0
    even_shares = row_count == 2 * LINES and 3 * block % LINES == 0
    if whole_blocks and col_count == 2 and even_shares:
        return live_units(ancestor_inverse, factor_panels, *others)
    return whole_panels(ancestor_inverse, factor_panels, *others)


def solution(mesh):
    return jax.shard_map(
        per_device,
        mesh=mesh,
        in_specs=(
            P(None, ("pole", "row"), "col"),
            P(None, None, ("pole", "col", "row"), None),
            P("pole", None, None, None),
            P("pole", None, None, None),
            P(),
            P(),
        ),
        out_specs=(
            P(None, None, ("pole", "row"), None),
            P("pole", None, None, None),
            P("pole", None, None, None),
        ),
        check_vma=False,
    )
```

profile of v0, /device:TPU:0, one launch (start us, length us, event | category | flops | bytes accessed | tf_op | source)
XLA Modules:
  0.0 340.4 jit_solution(11904180366998957337)
XLA Ops:
  7.2 2.9 make_plan.1.plan
  12.7 3.9 %compact_units.1 = (f32[20,2,128,128]{3,2,1,0:T(8,128)S(1)}, f32[4,2,128,128]{3,2,1,0:T(8,128)}) custom-call(s32[475]{0:T(512)S(1)} %make_plan.1.plan, s32[4]{0:T(128)S(1)} %copy-done.2, f32[4,2,768,128]{3,2,1,0:T(8,128)S(1)} %copy-done), custom_call_target="tpu_custom_call" | custom-call | tf_op jit(solution)/shard_map/compact_units/pallas_call | solution.py:182
  16.7 6.5 %collective-permute-start = (f32[20,2,128,128]{3,2,1,0:T(8,128)S(1)}, f32[20,2,128,128]{3,2,1,0:T(8,128)}, u32[]{:S(2)}, u32[]{:S(2)}) collective-permute-start(f32[20,2,128,128]{3,2,1,0:T(8,128)S(1)} %get-tuple-element.80.refs_1_.refs_0_), channel_id=1, source_target_pairs={{0,4},{2,6},{4,8},{6,10},{8,12},{10,14},{1,5},{3,7},{5,9},{7,11},{... | collective-permute-start | bytes 7864328 | tf_op jit(solution)/shard_map/ppermute | solution.py:574
  27.2 16.5 %gemm_units.6 = f32[4,1536,256]{2,1,0:T(8,128)} custom-call(s32[475]{0:T(512)S(1)} %make_plan.1.plan, s32[2]{0:T(128)S(1)} %pad_add_fusion.place, f32[2,1536,6144]{2,1,0:T(8,128)} %refs_1_.7, f32[20,2,128,128]{3,2,1,0:T(8,128)S(1)} %get-tuple-element.80.refs_1_.refs_0_), custom_call_target="tpu_custom_call" | custom-call | flops 7247757312 | bytes 22020096 | tf_op jit(solution)/shard_map/gemm_units/pallas_call | solution.py:311
  43.7 34.0 %collective-permute-done.refs_2_.refs_1_ = f32[20,2,128,128]{3,2,1,0:T(8,128)} collective-permute-done((f32[20,2,128,128]{3,2,1,0:T(8,128)S(1)}, f32[20,2,128,128]{3,2,1,0:T(8,128)}, u32[]{:S(2)}, u32[]{:S(2)}) %collective-permute-start) | collective-permute-done | bytes 2621472 | tf_op jit(solution)/shard_map/ppermute | solution.py:574
  77.7 5.8 %collective-permute-done.1.refs_3_.refs_2_ = f32[20,2,128,128]{3,2,1,0:T(8,128)} collective-permute-done((f32[20,2,128,128]{3,2,1,0:T(8,128)S(1)}, f32[20,2,128,128]{3,2,1,0:T(8,128)}, u32[]{:S(2)}, u32[]{:S(2)}) %collective-permute-start.1) | collective-permute-done | bytes 2621472 | tf_op jit(solution)/shard_map/ppermute | solution.py:574
  87.0 3.7 %broadcast_select_fusion.1 = f32[20,2,128,128]{3,2,1,0:T(8,128)} fusion(f32[20,2,128,128]{3,2,1,0:T(8,128)} %collective-permute-done.1.refs_3_.refs_2_, f32[20,2,128,128]{3,2,1,0:T(8,128)} %collective-permute-done.refs_2_.refs_1_, pred[]{:T(512)S(6)} %lt.82), kind=kLoop, calls=%fused_computation.2 | loop fusion | flops 655360 | bytes 7864321 | tf_op jit(solution)/shard_map/jit(_where)/select_n | solution.py:635
  92.2 7.2 %collective-permute-start.5 = (f32[20,2,128,128]{3,2,1,0:T(8,128)}, f32[20,2,128,128]{3,2,1,0:T(8,128)}, u32[]{:S(2)}, u32[]{:S(2)}) collective-permute-start(f32[20,2,128,128]{3,2,1,0:T(8,128)} %collective-permute-done.2.refs_4_.refs_3_), channel_id=1, source_target_pairs={{0,4},{2,6},{12,8},{14,10},{1,5},{3,7},{13,9},{15,11},{16,20},{18,... | collective-permute-start | bytes 7864328 | tf_op jit(solution)/shard_map/ppermute | solution.py:651
  99.4 2.6 broadcast_in_dim.19
  102.0 41.6 %gemm_units.7.refs_0_ = f32[4,1536,256]{2,1,0:T(8,128)} custom-call(s32[475]{0:T(512)S(1)} %get-tuple-element.237, s32[2]{0:T(128)S(1)} %get-tuple-element.253, f32[4,1536,256]{2,1,0:T(8,128)} %get-tuple-element.86.refs_0_, f32[2,1536,6144]{2,1,0:T(8,128)} %refs_1_.7, ...), custom_call_target="tpu_custom_call", output_to_operand_aliasing={{}: (2, {})} | custom-call | flops 21743271936 | bytes 40894464 | tf_op jit(solution)/shard_map/gemm_units/pallas_call | solution.py:311
  143.6 4.8 %collective-permute-done.6.refs_5_.refs_7_ = f32[20,2,128,128]{3,2,1,0:T(8,128)} collective-permute-done((f32[20,2,128,128]{3,2,1,0:T(8,128)}, f32[20,2,128,128]{3,2,1,0:T(8,128)}, u32[]{:S(2)}, u32[]{:S(2)}) %collective-permute-start.6) | collective-permute-done | bytes 2621472 | tf_op jit(solution)/shard_map/ppermute | solution.py:578
  148.4 3.8 %collective-permute-done.5.refs_4_.refs_6_ = f32[20,2,128,128]{3,2,1,0:T(8,128)} collective-permute-done((f32[20,2,128,128]{3,2,1,0:T(8,128)}, f32[20,2,128,128]{3,2,1,0:T(8,128)}, u32[]{:S(2)}, u32[]{:S(2)}) %collective-permute-start.5) | collective-permute-done | bytes 2621472 | tf_op jit(solution)/shard_map/ppermute | solution.py:651
  157.2 35.4 %gemm_units.8.refs_0_ = f32[4,1536,256]{2,1,0:T(8,128)} custom-call(s32[475]{0:T(512)S(1)} %get-tuple-element.237, s32[2]{0:T(128)S(1)} %get-tuple-element.253, f32[4,1536,256]{2,1,0:T(8,128)} %gemm_units.7.refs_0_, f32[2,1536,6144]{2,1,0:T(8,128)} %refs_1_.7, ...), custom_call_target="tpu_custom_call", output_to_operand_aliasing={{}: (2, {})} | custom-call | flops 28991029248 | bytes 50331648 | tf_op jit(solution)/shard_map/gemm_units/pallas_call | solution.py:311
  192.7 19.7 %collective-permute-done.9.refs_4_.refs_10_ = f32[20,2,128,128]{3,2,1,0:T(8,128)S(1)} collective-permute-done((f32[20,2,128,128]{3,2,1,0:T(8,128)S(1)}, f32[20,2,128,128]{3,2,1,0:T(8,128)S(1)}, u32[]{:S(2)}, u32[]{:S(2)}) %collective-permute-start.9) | collective-permute-done | bytes 2621472 | tf_op jit(solution)/shard_map/ppermute | solution.py:578
  217.5 30.2 %gemm_units.9.refs_0_ = f32[4,1536,256]{2,1,0:T(8,128)} custom-call(s32[475]{0:T(512)S(1)} %get-tuple-element.237, s32[2]{0:T(128)S(1)} %get-tuple-element.253, f32[4,1536,256]{2,1,0:T(8,128)} %gemm_units.8.refs_0_, f32[2,1536,6144]{2,1,0:T(8,128)} %refs_1_.7, ...), custom_call_target="tpu_custom_call", output_to_operand_aliasing={{}: (2, {})} | custom-call | flops 21743271936 | bytes 40894464 | tf_op jit(solution)/shard_map/gemm_units/pallas_call | solution.py:311
  247.7 5.3 %find_windows.1.near = f32[2,24,2,128,128]{4,3,2,1,0:T(8,128)} custom-call(s32[475]{0:T(512)S(1)} %get-tuple-element.237, s32[2]{0:T(128)S(1)} %get-tuple-element.253, f32[20,2,128,128]{3,2,1,0:T(8,128)S(1)} %get-tuple-element.80.refs_1_.refs_0_, f32[20,2,128,128]{3,2,1,0:T(8,128)} %collective-permute-done.refs_2_.refs_1_, ...), custom_call_target="tpu_custom_call" | custom-call | tf_op jit(solution)/shard_map/find_windows/pallas_call | solution.py:376
  253.1 22.7 %gemm_units.10.mine = f32[4,1536,256]{2,1,0:T(8,128)} custom-call(s32[475]{0:T(512)S(1)} %get-tuple-element.237, s32[2]{0:T(128)S(1)} %get-tuple-element.253, f32[4,1536,256]{2,1,0:T(8,128)} %gemm_units.9.refs_0_, f32[2,1536,6144]{2,1,0:T(8,128)} %refs_1_.7, f32[10,2,128,128]{3,2,1,0:T(8,128)S(1)} %collective-permute-done.12.refs_2_, ...), custom_call_target="tpu_custom_call", output_to_operand_aliasing={{}: (2, {})} | custom-call | flops 7247757312 | bytes 22020096 | tf_op jit(solution)/shard_map/gemm_units/pallas_call | solution.py:311
  276.0 10.5 %contract_windows.1 = f32[6,2,128,128]{3,2,1,0:T(8,128)S(1)} custom-call(s32[475]{0:T(512)S(1)} %get-tuple-element.237, s32[2]{0:T(128)S(1)} %get-tuple-element.253, f32[4,1536,256]{2,1,0:T(8,128)} %gemm_units.10.mine, f32[2,24,2,128,128]{4,3,2,1,0:T(8,128)} %find_windows.1.near, f32[2,24,2,128,128]{4,3,2,1,0:T(8,128)} %collective-permute-done.14.far), custom_call_target="tpu_custom_call" | custom-call | tf_op jit(solution)/shard_map/contract_windows/pallas_call | solution.py:445
  288.6 5.5 %collective-permute-start.16 = (f32[4,96,128]{2,1,0:T(8,128)S(1)}, f32[4,96,128]{2,1,0:T(8,128)S(1)}, u32[]{:S(2)}, u32[]{:S(2)}) collective-permute-start(f32[4,96,128]{2,1,0:T(8,128)S(1)} %dynamic-slice_bitcast_fusion.1), channel_id=1, source_target_pairs={{0,2},{2,0},{4,6},{6,4},{8,10},{10,8},{12,14},{14,12},{1,3},{3,1},... | collective-permute-start | bytes 589832 | tf_op jit(solution)/shard_map/ppermute | solution.py:578
  294.1 6.6 %finish_columns.2.refs_0_ = f32[4,2,1536,128]{3,2,1,0:T(8,128)} custom-call(s32[475]{0:T(512)S(1)} %get-tuple-element.237, s32[4]{0:T(128)S(1)} %copy-done.3, f32[4,1536,256]{2,1,0:T(8,128)} %gemm_units.10.mine, f32[4,1536,256]{2,1,0:T(8,128)} %collective-permute-done.13.other, f32[2,2,128,128]{3,2,1,0:T(8,128)S(1)} %copy-done.1), custom_call_target="tpu_custom_call" | custom-call | flops 603979776 | bytes 9437184 | tf_op jit(solution)/shard_map/finish_columns/pallas_call | solution.py:510
  300.9 6.8 %collective-permute-start.18 = (f32[96,128]{1,0:T(8,128)S(1)}, f32[96,128]{1,0:T(8,128)S(1)}, u32[]{:S(2)}, u32[]{:S(2)}) collective-permute-start(f32[96,128]{1,0:T(8,128)S(1)} %get-tuple-element.139), channel_id=1, source_target_pairs={{0,8},{2,10},{4,12},{6,14},{8,0},{10,2},{12,4},{14,6},{1,9},{3,11}... | collective-permute-start | bytes 147464 | tf_op jit(solution)/shard_map/ppermute | solution.py:598
  307.7 6.6 %finish_columns.3 = f32[4,2,1536,128]{3,2,1,0:T(8,128)} custom-call(s32[475]{0:T(512)S(1)} %get-tuple-element.237, s32[4]{0:T(128)S(1)} %copy-done.3, f32[4,1536,256]{2,1,0:T(8,128)} %gemm_units.10.mine, f32[4,1536,256]{2,1,0:T(8,128)} %collective-permute-done.13.other, f32[2,2,128,128]{3,2,1,0:T(8,128)S(1)} %copy-done.1, ...), custom_call_target="tpu_custom_call", output_to_operand_aliasing={{}: (5, {})} | custom-call | flops 603979776 | bytes 9437184 | tf_op jit(solution)/shard_map/finish_columns/pallas_call | solution.py:510
  322.5 5.1 %collective-permute-done.23 = f32[4,96,128]{2,1,0:T(8,128)S(1)} collective-permute-done((f32[4,96,128]{2,1,0:T(8,128)S(1)}, f32[4,96,128]{2,1,0:T(8,128)S(1)}, u32[]{:S(2)}, u32[]{:S(2)}) %collective-permute-start.23) | collective-permute-done | bytes 196640 | tf_op jit(solution)/shard_map/ppermute | solution.py:578
  330.5 3.0 finish_diagonals.1
  (68 shorter events, 34.5 us)
Async XLA Ops:
  16.7 61.0 %collective-permute-start = (f32[20,2,128,128]{3,2,1,0:T(8,128)S(1)}, f32[20,2,128,128]{3,2,1,0:T(8,128)}, u32[]{:S(2)}, u32[]{:S(2)}) collective-permute-start(f32[20,2,128,128]{3,2,1,0:T(8,128)S(1)} %get-tuple-element.80.refs_1_.refs_0_), channel_id=1, source_target_pairs={{0,4},{2,6},{4,8},{6,10},{8,12},{10,14},{1,5},{3,7},{5,9},{7,11},{... | collective-permute-start | bytes 7864328 | tf_op jit(solution)/shard_map/ppermute | solution.py:574
  23.2 60.3 %collective-permute-start.1 = (f32[20,2,128,128]{3,2,1,0:T(8,128)S(1)}, f32[20,2,128,128]{3,2,1,0:T(8,128)}, u32[]{:S(2)}, u32[]{:S(2)}) collective-permute-start(f32[20,2,128,128]{3,2,1,0:T(8,128)S(1)} %get-tuple-element.80.refs_1_.refs_0_), channel_id=1, source_target_pairs={{4,0},{6,2},{8,4},{10,6},{12,8},{14,10},{5,1},{7,3},{9,5},{11,7},{... | collective-permute-start | bytes 7864328 | tf_op jit(solution)/shard_map/ppermute | solution.py:574
  24.5 59.0 %collective-permute-start.2 = (f32[20,2,128,128]{3,2,1,0:T(8,128)S(1)}, f32[20,2,128,128]{3,2,1,0:T(8,128)}, u32[]{:S(2)}, u32[]{:S(2)}) collective-permute-start(f32[20,2,128,128]{3,2,1,0:T(8,128)S(1)} %get-tuple-element.80.refs_1_.refs_0_), channel_id=1, source_target_pairs={{0,2},{2,0},{4,6},{6,4},{8,10},{10,8},{12,14},{14,12},{1,3},{3,1},... | collective-permute-start | bytes 7864328 | tf_op jit(solution)/shard_map/ppermute | solution.py:578
  83.5 64.9 %collective-permute-start.3 = (f32[20,2,128,128]{3,2,1,0:T(8,128)}, f32[20,2,128,128]{3,2,1,0:T(8,128)}, u32[]{:S(2)}, u32[]{:S(2)}) collective-permute-start(f32[20,2,128,128]{3,2,1,0:T(8,128)} %collective-permute-done.refs_2_.refs_1_), channel_id=1, source_target_pairs={{4,8},{6,10},{8,12},{10,14},{5,9},{7,11},{9,13},{11,15},{20,24},{2... | collective-permute-start | bytes 7864328 | tf_op jit(solution)/shard_map/ppermute | solution.py:574
  85.7 62.8 %collective-permute-start.4 = (f32[20,2,128,128]{3,2,1,0:T(8,128)}, f32[20,2,128,128]{3,2,1,0:T(8,128)}, u32[]{:S(2)}, u32[]{:S(2)}) collective-permute-start(f32[20,2,128,128]{3,2,1,0:T(8,128)} %collective-permute-done.1.refs_3_.refs_2_), channel_id=1, source_target_pairs={{4,0},{6,2},{8,4},{10,6},{5,1},{7,3},{9,5},{11,7},{20,16},{22,18},... | collective-permute-start | bytes 7864328 | tf_op jit(solution)/shard_map/ppermute | solution.py:574
  90.7 57.7 %collective-permute-start.6 = (f32[20,2,128,128]{3,2,1,0:T(8,128)}, f32[20,2,128,128]{3,2,1,0:T(8,128)}, u32[]{:S(2)}, u32[]{:S(2)}) collective-permute-start(f32[20,2,128,128]{3,2,1,0:T(8,128)} %broadcast_select_fusion.1), channel_id=1, source_target_pairs={{0,2},{2,0},{4,6},{6,4},{8,10},{10,8},{12,14},{14,12},{1,3},{3,1},... | collective-permute-start | bytes 7864328 | tf_op jit(solution)/shard_map/ppermute | solution.py:578
  92.2 60.0 %collective-permute-start.5 = (f32[20,2,128,128]{3,2,1,0:T(8,128)}, f32[20,2,128,128]{3,2,1,0:T(8,128)}, u32[]{:S(2)}, u32[]{:S(2)}) collective-permute-start(f32[20,2,128,128]{3,2,1,0:T(8,128)} %collective-permute-done.2.refs_4_.refs_3_), channel_id=1, source_target_pairs={{0,4},{2,6},{12,8},{14,10},{1,5},{3,7},{13,9},{15,11},{16,20},{18,... | collective-permute-start | bytes 7864328 | tf_op jit(solution)/shard_map/ppermute | solution.py:651
  152.3 60.1 %collective-permute-start.7 = (f32[20,2,128,128]{3,2,1,0:T(8,128)}, f32[20,2,128,128]{3,2,1,0:T(8,128)S(1)}, u32[]{:S(2)}, u32[]{:S(2)}) collective-permute-start(f32[20,2,128,128]{3,2,1,0:T(8,128)} %collective-permute-done.3.refs_2_.refs_4_), channel_id=1, source_target_pairs={{8,12},{10,14},{9,13},{11,15},{24,28},{26,30},{25,29},{27,31}} | collective-permute-start | bytes 7864328 | tf_op jit(solution)/shard_map/ppermute | solution.py:574
  155.3 58.7 %collective-permute-start.8 = (f32[20,2,128,128]{3,2,1,0:T(8,128)}, f32[20,2,128,128]{3,2,1,0:T(8,128)S(1)}, u32[]{:S(2)}, u32[]{:S(2)}) collective-permute-start(f32[20,2,128,128]{3,2,1,0:T(8,128)} %collective-permute-done.4.refs_3_.refs_5_), channel_id=1, source_target_pairs={{4,0},{6,2},{5,1},{7,3},{20,16},{22,18},{21,17},{23,19}} | collective-permute-start | bytes 7864328 | tf_op jit(solution)/shard_map/ppermute | solution.py:574
  156.6 55.7 %collective-permute-start.9 = (f32[20,2,128,128]{3,2,1,0:T(8,128)S(1)}, f32[20,2,128,128]{3,2,1,0:T(8,128)S(1)}, u32[]{:S(2)}, u32[]{:S(2)}) collective-permute-start(f32[20,2,128,128]{3,2,1,0:T(8,128)S(1)} %broadcast_select_fusion), channel_id=1, source_target_pairs={{0,2},{2,0},{4,6},{6,4},{8,10},{10,8},{12,14},{14,12},{1,3},{3,1},... | collective-permute-start | bytes 7864328 | tf_op jit(solution)/shard_map/ppermute | solution.py:578
  214.2 38.9 %collective-permute-start.10 = (f32[10,2,128,128]{3,2,1,0:T(8,128)S(1)}, f32[10,2,128,128]{3,2,1,0:T(8,128)S(1)}, u32[]{:S(2)}, u32[]{:S(2)}) collective-permute-start(f32[10,2,128,128]{3,2,1,0:T(8,128)S(1)} %slice.10), channel_id=1, source_target_pairs={{8,12},{10,14},{9,13},{11,15},{24,28},{26,30},{25,29},{27,31}} | collective-permute-start | bytes 3932168 | tf_op jit(solution)/shard_map/ppermute | solution.py:574
  214.9 38.2 %collective-permute-start.11 = (f32[10,2,128,128]{3,2,1,0:T(8,128)S(1)}, f32[10,2,128,128]{3,2,1,0:T(8,128)S(1)}, u32[]{:S(2)}, u32[]{:S(2)}) collective-permute-start(f32[10,2,128,128]{3,2,1,0:T(8,128)S(1)} %slice.10), channel_id=1, source_target_pairs={{4,0},{6,2},{5,1},{7,3},{20,16},{22,18},{21,17},{23,19}} | collective-permute-start | bytes 3932168 | tf_op jit(solution)/shard_map/ppermute | solution.py:574
  217.5 35.6 %collective-permute-start.12 = (f32[10,2,128,128]{3,2,1,0:T(8,128)}, f32[10,2,128,128]{3,2,1,0:T(8,128)S(1)}, u32[]{:S(2)}, u32[]{:S(2)}) collective-permute-start(f32[10,2,128,128]{3,2,1,0:T(8,128)} %slice_select_fusion), channel_id=1, source_target_pairs={{0,2},{2,0},{4,6},{6,4},{8,10},{10,8},{12,14},{14,12},{1,3},{3,1},... | collective-permute-start | bytes 3932168 | tf_op jit(solution)/shard_map/ppermute | solution.py:578
  253.0 23.0 %collective-permute-start.14 = (f32[2,24,2,128,128]{4,3,2,1,0:T(8,128)}, f32[2,24,2,128,128]{4,3,2,1,0:T(8,128)}, u32[]{:S(2)}, u32[]{:S(2)}) collective-permute-start(f32[2,24,2,128,128]{4,3,2,1,0:T(8,128)} %find_windows.1.near), channel_id=1, source_target_pairs={{0,1},{1,0},{2,3},{3,2},{4,5},{5,4},{6,7},{7,6},{8,9},{9,8},{10,11... | collective-permute-start | bytes 18874376 | tf_op jit(solution)/shard_map/ppermute | solution.py:578
  275.9 10.6 %collective-permute-start.13 = (f32[4,1536,256]{2,1,0:T(8,128)}, f32[4,1536,256]{2,1,0:T(8,128)}, u32[]{:S(2)}, u32[]{:S(2)}) collective-permute-start(f32[4,1536,256]{2,1,0:T(8,128)} %gemm_units.10.mine), channel_id=1, source_target_pairs={{0,1},{1,0},{2,3},{3,2},{4,5},{5,4},{6,7},{7,6},{8,9},{9,8},{10,11... | collective-permute-start | bytes 18874376 | tf_op jit(solution)/shard_map/ppermute | solution.py:578
  286.5 2.0 collective-permute-start.15
  288.6 12.2 %collective-permute-start.16 = (f32[4,96,128]{2,1,0:T(8,128)S(1)}, f32[4,96,128]{2,1,0:T(8,128)S(1)}, u32[]{:S(2)}, u32[]{:S(2)}) collective-permute-start(f32[4,96,128]{2,1,0:T(8,128)S(1)} %dynamic-slice_bitcast_fusion.1), channel_id=1, source_target_pairs={{0,2},{2,0},{4,6},{6,4},{8,10},{10,8},{12,14},{14,12},{1,3},{3,1},... | collective-permute-start | bytes 589832 | tf_op jit(solution)/shard_map/ppermute | solution.py:578
  300.8 13.5 %collective-permute-start.17 = (f32[96,128]{1,0:T(8,128)S(1)}, f32[96,128]{1,0:T(8,128)S(1)}, u32[]{:S(2)}, u32[]{:S(2)}) collective-permute-start(f32[96,128]{1,0:T(8,128)S(1)} %get-tuple-element.140), channel_id=1, source_target_pairs={{0,4},{2,6},{4,8},{6,10},{8,12},{10,14},{12,0},{14,2},{1,5},{3,7},... | collective-permute-start | bytes 147464 | tf_op jit(solution)/shard_map/ppermute | solution.py:598
  300.9 13.4 %collective-permute-start.18 = (f32[96,128]{1,0:T(8,128)S(1)}, f32[96,128]{1,0:T(8,128)S(1)}, u32[]{:S(2)}, u32[]{:S(2)}) collective-permute-start(f32[96,128]{1,0:T(8,128)S(1)} %get-tuple-element.139), channel_id=1, source_target_pairs={{0,8},{2,10},{4,12},{6,14},{8,0},{10,2},{12,4},{14,6},{1,9},{3,11}... | collective-permute-start | bytes 147464 | tf_op jit(solution)/shard_map/ppermute | solution.py:598
  307.7 6.6 %collective-permute-start.19 = (f32[96,128]{1,0:T(8,128)S(1)}, f32[96,128]{1,0:T(8,128)S(1)}, u32[]{:S(2)}, u32[]{:S(2)}) collective-permute-start(f32[96,128]{1,0:T(8,128)S(1)} %get-tuple-element.138), channel_id=1, source_target_pairs={{0,12},{2,14},{4,0},{6,2},{8,4},{10,6},{12,8},{14,10},{1,13},{3,15... | collective-permute-start | bytes 147464 | tf_op jit(solution)/shard_map/ppermute | solution.py:598
  314.3 6.4 %collective-permute-start.20 = (f32[96,128]{1,0:T(8,128)S(1)}, f32[96,128]{1,0:T(8,128)S(1)}, u32[]{:S(2)}, u32[]{:S(2)}) collective-permute-start(f32[96,128]{1,0:T(8,128)S(1)} %get-tuple-element.133), channel_id=1, source_target_pairs={{0,4},{2,6},{4,8},{6,10},{8,12},{10,14},{12,0},{14,2},{1,5},{3,7},... | collective-permute-start | bytes 147464 | tf_op jit(solution)/shard_map/ppermute | solution.py:598
  316.4 5.4 %collective-permute-start.21 = (f32[96,128]{1,0:T(8,128)S(1)}, f32[96,128]{1,0:T(8,128)S(1)}, u32[]{:S(2)}, u32[]{:S(2)}) collective-permute-start(f32[96,128]{1,0:T(8,128)S(1)} %get-tuple-element.133), channel_id=1, source_target_pairs={{0,8},{2,10},{4,12},{6,14},{8,0},{10,2},{12,4},{14,6},{1,9},{3,11}... | collective-permute-start | bytes 147464 | tf_op jit(solution)/shard_map/ppermute | solution.py:598
  316.4 5.4 %collective-permute-start.22 = (f32[96,128]{1,0:T(8,128)S(1)}, f32[96,128]{1,0:T(8,128)S(1)}, u32[]{:S(2)}, u32[]{:S(2)}) collective-permute-start(f32[96,128]{1,0:T(8,128)S(1)} %get-tuple-element.133), channel_id=1, source_target_pairs={{0,12},{2,14},{4,0},{6,2},{8,4},{10,6},{12,8},{14,10},{1,13},{3,15... | collective-permute-start | bytes 147464 | tf_op jit(solution)/shard_map/ppermute | solution.py:598
  321.9 5.7 %collective-permute-start.23 = (f32[4,96,128]{2,1,0:T(8,128)S(1)}, f32[4,96,128]{2,1,0:T(8,128)S(1)}, u32[]{:S(2)}, u32[]{:S(2)}) collective-permute-start(f32[4,96,128]{2,1,0:T(8,128)S(1)} %bitcast_dynamic-update-slice_fusion), channel_id=1, source_target_pairs={{0,2},{2,0},{4,6},{6,4},{8,10},{10,8},{12,14},{14,12},{1,3},{3,1},... | collective-permute-start | bytes 589832 | tf_op jit(solution)/shard_map/ppermute | solution.py:578
  (5 other events, 30.2 us)
where the time goes:
time: 341 us; the launch traced here: 340 us
  Pallas kernels  185 us (54%)
  waiting for transfers between devices  80.9 us (24%)
  starting transfers between devices  44.7 us (13%)
  between operations  14.9 us (4%)
  other arithmetic  8.51 us (2%)
  local copies, waits for them, and re-layouts  5.95 us (2%)
    pallas_call x5, Pallas kernels, gemm_units(): pl.pallas_call(functools.partial(gemm_kernel, layout, which, parted, firs...  146 us
    ppermute x8, waiting for transfers between devices, along(): return lax.ppermute(value, 'row', route)  41.5 us
    ppermute x10, waiting for transfers between devices, swap(): lax.ppermute(value, axis, [(at, at ^ 1) for at in range(lax.axis_size(axi...  32.7 us
    ppermute x8, starting transfers between devices, along(): return lax.ppermute(value, 'row', route)  15.4 us
    pallas_call x2, Pallas kernels, finish_columns(): pl.pallas_call(functools.partial(column_kernel, layout, step_blocks, firs...  13.2 us
    ppermute x6, starting transfers between devices, turn(): return lax.ppermute(value, 'row', route)  11.4 us
    ppermute x10, starting transfers between devices, swap(): lax.ppermute(value, axis, [(at, at ^ 1) for at in range(lax.axis_size(axi...  10.7 us
    pallas_call x1, Pallas kernels, contract_windows(): pl.pallas_call(functools.partial(contract_kernel, layout, step_blocks), o...  10.5 us
  transfers between devices with their start and end apart: 25, of which 11 were waited for; matrix products, arithmetic and copies ran while one was open for 3% of the time, Pallas kernels for 52%

commit v1 on v0

--- a/solution.py
+++ b/solution.py
@@ -212,6 +212,7 @@
     step = pl.program_id(0)
     block, rows = layout.block, layout.tile_rows
     width = 2 * block
+    span_rows = layout.group * block
 
     def each_slot(source, target, act):
         for slot in range(layout.slots):
@@ -220,7 +221,7 @@
     @pl.when(step == 0)
     def _():
         if first_call:
-            total[...] = jnp.zeros_like(total)
+            total[: layout.slots] = jnp.zeros((layout.slots, rows, width), jnp.float32)
         else:
             each_slot(in_ref, total, "start")
 
@@ -241,7 +242,7 @@
         def _():
             each_slot(in_ref, total, "wait")
 
-    base = place[1] * layout.rows * layout.units + owner * layout.units
+    base = place[1] * layout.rows * layout.units + jnp.maximum(owner, 0) * layout.units
     base = base + step % layout.piece_blocks * layout.slots
     front = units[0].shape[0]
 
@@ -263,31 +264,50 @@
             found.append((here, lambda ref=ref: ref.at[rank]))
         return found
 
-    @pl.loop(0, jnp.where(owner >= 0, layout.slots, 0))
-    def _(slot):
+    count = jnp.int32(0)
+    chosen = [jnp.int32(layout.slots)] * layout.slots
+    for slot in range(layout.slots):
         rank = plan[layout.ranks + base + slot]
-        if which is None:
-            wanted = rank >= layout.room
-        else:
-            wanted = (rank >= 0) & (rank < layout.room)
-
-        for here, find in places(rank):
-
-            @pl.when(here)
-            def _():
-                unit = find()
-                real, imag = unit[0], unit[1]
-                real_parts, imag_parts = halves(real), halves(imag)
-                for third, part in enumerate((0, 0, 1)):
-                    top = third * width
-                    weights[top : top + block, :block] = real_parts[part]
-                    weights[top : top + block, block:] = imag_parts[part]
-                    weights[top + block : top + width, :block] = -imag_parts[part]
-                    weights[top + block : top + width, block:] = real_parts[part]
-
-        @pl.when(wanted & (plan[layout.live + slot] > 0))
-        def _():
-            total[slot] += dot32(a_parts[...], weights[...])
+        wanted = rank >= layout.room if which is None else (rank >= 0) & (rank < layout.room)
+        wanted = wanted & (owner >= 0) & (plan[layout.live + slot] > 0)
+        for at in range(layout.slots):
+            chosen[at] = jnp.where(wanted & (count == at), slot, chosen[at])
+        count = count + wanted.astype(jnp.int32)
+
+    @pl.loop(0, (count + 1) // 2)
+    def _(pair):
+        slots = []
+        for side in range(2):
+            slot = chosen[side]
+            for at in range(2 + side, layout.slots, 2):
+                slot = jnp.where(pair == at // 2, chosen[at], slot)
+            slots.append(slot)
+            used = slot < layout.slots
+            rank = plan[layout.ranks + base + jnp.minimum(slot, layout.slots - 1)]
+            left = slice(side * width, side * width + block)
+            middle = slice(side * width + block, (side + 1) * width)
+
+            for here, find in places(rank):
+
+                @pl.when(used & here)
+                def _():
+                    unit = find()
+                    real, imag = unit[0], unit[1]
+                    real_parts, imag_parts = halves(real), halves(imag)
+                    for third, part in enumerate((0, 0, 1)):
+                        upper = slice(third * width, third * width + block)
+                        lower = slice(third * width + block, (third + 1) * width)
+                        weights[upper, left] = real_parts[part]
+                        weights[upper, middle] = imag_parts[part]
+                        weights[lower, left] = -imag_parts[part]
+                        weights[lower, middle] = real_parts[part]
+
+        @pl.loop(0, rows // span_rows)
+        def _(index):
+            span = pl.ds(pl.multiple_of(index * span_rows, span_rows), span_rows)
+            product = dot32(a_parts[span, :], weights[...])
+            for side in range(2):
+                total[slots[side], span, :] += product[:, side * width : (side + 1) * width]
 
     @pl.when(step == pl.num_programs(0) - 1)
     def _():
@@ -326,9 +346,9 @@
             ],
             out_specs=hbm,
             scratch_shapes=[
-                pltpu.VMEM(shape, jnp.float32),
+                pltpu.VMEM((layout.slots + 1, rows, width), jnp.float32),
                 pltpu.VMEM((rows, 3 * width), jnp.bfloat16),
-                pltpu.VMEM((3 * width, width), jnp.bfloat16),
+                pltpu.VMEM((3 * width, 2 * width), jnp.bfloat16),
                 pltpu.SemaphoreType.DMA((layout.slots,)),
             ],
         ),

time: 341 us -> 366 us (1.073)
  Pallas kernels: 185 us -> 226 us
  waiting for transfers between devices: 80.9 us -> 67.5 us
  starting transfers between devices: 44.7 us -> 40.9 us
    pallas_call x5, Pallas kernels: 146 us -> 187 us  [gemm_units(): pl.pallas_call(functools.partial(gemm_kernel, layout, which, parted, firs...]
    ppermute x10, waiting for transfers between devices: 32.7 us -> 15.1 us  [swap(): lax.ppermute(value, axis, [(at, at ^ 1) for at in range(lax.axis_size(axi...]
    ppermute x8, waiting for transfers between devices: 41.5 us -> 46.3 us  [along(): return lax.ppermute(value, 'row', route)]
  transfers between devices with their start and end apart: 25 -> 25, of which waited for: 11 -> 11; matrix products, arithmetic and copies ran while one was open for 3% -> 3% of each run, Pallas kernels for 52% -> 59%
where the time goes in v1:
time: 366 us; the launch traced here: 364 us
  Pallas kernels  226 us (62%)
  waiting for transfers between devices  67.5 us (18%)
  starting transfers between devices  40.9 us (11%)
  between operations  14.9 us (4%)
  other arithmetic  8.51 us (2%)
  local copies, waits for them, and re-layouts  5.95 us (2%)
    pallas_call x5, Pallas kernels, gemm_units(): pl.pallas_call(functools.partial(gemm_kernel, layout, which, parted, firs...  187 us
    ppermute x8, waiting for transfers between devices, along(): return lax.ppermute(value, 'row', route)  46.3 us
    ppermute x8, starting transfers between devices, along(): return lax.ppermute(value, 'row', route)  15.4 us
    ppermute x10, waiting for transfers between devices, swap(): lax.ppermute(value, axis, [(at, at ^ 1) for at in range(lax.axis_size(axi...  15.1 us
    pallas_call x2, Pallas kernels, finish_columns(): pl.pallas_call(functools.partial(column_kernel, layout, step_blocks, firs...  13.2 us
    pallas_call x1, Pallas kernels, contract_windows(): pl.pallas_call(functools.partial(contract_kernel, layout, step_blocks), o...  10.4 us
    ppermute x10, starting transfers between devices, swap(): lax.ppermute(value, axis, [(at, at ^ 1) for at in range(lax.axis_size(axi...  9.53 us
    ppermute x6, starting transfers between devices, turn(): return lax.ppermute(value, 'row', route)  8.87 us
  transfers between devices with their start and end apart: 25, of which 11 were waited for; matrix products, arithmetic and copies ran while one was open for 3% of the time, Pallas kernels for 59%

profile of v1, /device:TPU:0, one launch (start us, length us, event | category | flops | bytes accessed | tf_op | source)
XLA Modules:
  0.0 364.2 jit_solution(14820846403512608992)
XLA Ops:
  7.2 2.9 make_plan.1.plan
  12.7 3.9 %compact_units.1 = (f32[20,2,128,128]{3,2,1,0:T(8,128)S(1)}, f32[4,2,128,128]{3,2,1,0:T(8,128)}) custom-call(s32[475]{0:T(512)S(1)} %make_plan.1.plan, s32[4]{0:T(128)S(1)} %copy-done.2, f32[4,2,768,128]{3,2,1,0:T(8,128)S(1)} %copy-done), custom_call_target="tpu_custom_call" | custom-call | tf_op jit(solution)/shard_map/compact_units/pallas_call | solution.py:182
  16.7 6.5 %collective-permute-start = (f32[20,2,128,128]{3,2,1,0:T(8,128)S(1)}, f32[20,2,128,128]{3,2,1,0:T(8,128)}, u32[]{:S(2)}, u32[]{:S(2)}) collective-permute-start(f32[20,2,128,128]{3,2,1,0:T(8,128)S(1)} %get-tuple-element.80.refs_1_.refs_0_), channel_id=1, source_target_pairs={{0,4},{2,6},{4,8},{6,10},{8,12},{10,14},{1,5},{3,7},{5,9},{7,11},{... | collective-permute-start | bytes 7864328 | tf_op jit(solution)/shard_map/ppermute | solution.py:594
  27.2 23.5 %gemm_units.6 = f32[4,1536,256]{2,1,0:T(8,128)} custom-call(s32[475]{0:T(512)S(1)} %make_plan.1.plan, s32[2]{0:T(128)S(1)} %pad_add_fusion.place, f32[2,1536,6144]{2,1,0:T(8,128)} %refs_1_.7, f32[20,2,128,128]{3,2,1,0:T(8,128)S(1)} %get-tuple-element.80.refs_1_.refs_0_), custom_call_target="tpu_custom_call" | custom-call | flops 7247757312 | bytes 22020096 | tf_op jit(solution)/shard_map/gemm_units/pallas_call | solution.py:331
  50.7 27.0 %collective-permute-done.refs_2_.refs_1_ = f32[20,2,128,128]{3,2,1,0:T(8,128)} collective-permute-done((f32[20,2,128,128]{3,2,1,0:T(8,128)S(1)}, f32[20,2,128,128]{3,2,1,0:T(8,128)}, u32[]{:S(2)}, u32[]{:S(2)}) %collective-permute-start) | collective-permute-done | bytes 2621472 | tf_op jit(solution)/shard_map/ppermute | solution.py:594
  77.7 5.8 %collective-permute-done.1.refs_3_.refs_2_ = f32[20,2,128,128]{3,2,1,0:T(8,128)} collective-permute-done((f32[20,2,128,128]{3,2,1,0:T(8,128)S(1)}, f32[20,2,128,128]{3,2,1,0:T(8,128)}, u32[]{:S(2)}, u32[]{:S(2)}) %collective-permute-start.1) | collective-permute-done | bytes 2621472 | tf_op jit(solution)/shard_map/ppermute | solution.py:594
  87.0 3.7 %broadcast_select_fusion.1 = f32[20,2,128,128]{3,2,1,0:T(8,128)} fusion(f32[20,2,128,128]{3,2,1,0:T(8,128)} %collective-permute-done.1.refs_3_.refs_2_, f32[20,2,128,128]{3,2,1,0:T(8,128)} %collective-permute-done.refs_2_.refs_1_, pred[]{:T(512)S(6)} %lt.82), kind=kLoop, calls=%fused_computation.2 | loop fusion | flops 655360 | bytes 7864321 | tf_op jit(solution)/shard_map/jit(_where)/select_n | solution.py:655
  92.2 7.2 %collective-permute-start.5 = (f32[20,2,128,128]{3,2,1,0:T(8,128)}, f32[20,2,128,128]{3,2,1,0:T(8,128)}, u32[]{:S(2)}, u32[]{:S(2)}) collective-permute-start(f32[20,2,128,128]{3,2,1,0:T(8,128)} %collective-permute-done.2.refs_4_.refs_3_), channel_id=1, source_target_pairs={{0,4},{2,6},{12,8},{14,10},{1,5},{3,7},{13,9},{15,11},{16,20},{18,... | collective-permute-start | bytes 7864328 | tf_op jit(solution)/shard_map/ppermute | solution.py:671
  102.0 42.7 %gemm_units.7.refs_0_ = f32[4,1536,256]{2,1,0:T(8,128)} custom-call(s32[475]{0:T(512)S(1)} %get-tuple-element.237, s32[2]{0:T(128)S(1)} %get-tuple-element.253, f32[4,1536,256]{2,1,0:T(8,128)} %get-tuple-element.86.refs_0_, f32[2,1536,6144]{2,1,0:T(8,128)} %refs_1_.7, ...), custom_call_target="tpu_custom_call", output_to_operand_aliasing={{}: (2, {})} | custom-call | flops 21743271936 | bytes 40894464 | tf_op jit(solution)/shard_map/gemm_units/pallas_call | solution.py:331
  144.7 3.8 %collective-permute-done.6.refs_5_.refs_7_ = f32[20,2,128,128]{3,2,1,0:T(8,128)} collective-permute-done((f32[20,2,128,128]{3,2,1,0:T(8,128)}, f32[20,2,128,128]{3,2,1,0:T(8,128)}, u32[]{:S(2)}, u32[]{:S(2)}) %collective-permute-start.6) | collective-permute-done | bytes 2621472 | tf_op jit(solution)/shard_map/ppermute | solution.py:598
  148.4 3.8 %collective-permute-done.5.refs_4_.refs_6_ = f32[20,2,128,128]{3,2,1,0:T(8,128)} collective-permute-done((f32[20,2,128,128]{3,2,1,0:T(8,128)}, f32[20,2,128,128]{3,2,1,0:T(8,128)}, u32[]{:S(2)}, u32[]{:S(2)}) %collective-permute-start.5) | collective-permute-done | bytes 2621472 | tf_op jit(solution)/shard_map/ppermute | solution.py:671
  157.2 52.5 %gemm_units.8.refs_0_ = f32[4,1536,256]{2,1,0:T(8,128)} custom-call(s32[475]{0:T(512)S(1)} %get-tuple-element.237, s32[2]{0:T(128)S(1)} %get-tuple-element.253, f32[4,1536,256]{2,1,0:T(8,128)} %gemm_units.7.refs_0_, f32[2,1536,6144]{2,1,0:T(8,128)} %refs_1_.7, ...), custom_call_target="tpu_custom_call", output_to_operand_aliasing={{}: (2, {})} | custom-call | flops 28991029248 | bytes 50331648 | tf_op jit(solution)/shard_map/gemm_units/pallas_call | solution.py:331
  209.7 3.6 collective-permute-done.9.refs_4_.refs_10_
  213.3 13.4 %collective-permute-done.8.refs_3_.refs_9_ = f32[20,2,128,128]{3,2,1,0:T(8,128)S(1)} collective-permute-done((f32[20,2,128,128]{3,2,1,0:T(8,128)}, f32[20,2,128,128]{3,2,1,0:T(8,128)S(1)}, u32[]{:S(2)}, u32[]{:S(2)}) %collective-permute-start.8) | collective-permute-done | bytes 2621472 | tf_op jit(solution)/shard_map/ppermute | solution.py:594
  230.3 48.1 %gemm_units.9.refs_0_ = f32[4,1536,256]{2,1,0:T(8,128)} custom-call(s32[475]{0:T(512)S(1)} %get-tuple-element.237, s32[2]{0:T(128)S(1)} %get-tuple-element.253, f32[4,1536,256]{2,1,0:T(8,128)} %gemm_units.8.refs_0_, f32[2,1536,6144]{2,1,0:T(8,128)} %refs_1_.7, ...), custom_call_target="tpu_custom_call", output_to_operand_aliasing={{}: (2, {})} | custom-call | flops 21743271936 | bytes 40894464 | tf_op jit(solution)/shard_map/gemm_units/pallas_call | solution.py:331
  278.4 5.3 %find_windows.1.near = f32[2,24,2,128,128]{4,3,2,1,0:T(8,128)} custom-call(s32[475]{0:T(512)S(1)} %get-tuple-element.237, s32[2]{0:T(128)S(1)} %get-tuple-element.253, f32[20,2,128,128]{3,2,1,0:T(8,128)S(1)} %get-tuple-element.80.refs_1_.refs_0_, f32[20,2,128,128]{3,2,1,0:T(8,128)} %collective-permute-done.refs_2_.refs_1_, ...), custom_call_target="tpu_custom_call" | custom-call | tf_op jit(solution)/shard_map/find_windows/pallas_call | solution.py:396
  283.8 20.7 %gemm_units.10.mine = f32[4,1536,256]{2,1,0:T(8,128)} custom-call(s32[475]{0:T(512)S(1)} %get-tuple-element.237, s32[2]{0:T(128)S(1)} %get-tuple-element.253, f32[4,1536,256]{2,1,0:T(8,128)} %gemm_units.9.refs_0_, f32[2,1536,6144]{2,1,0:T(8,128)} %refs_1_.7, f32[10,2,128,128]{3,2,1,0:T(8,128)S(1)} %collective-permute-done.12.refs_2_, ...), custom_call_target="tpu_custom_call", output_to_operand_aliasing={{}: (2, {})} | custom-call | flops 7247757312 | bytes 22020096 | tf_op jit(solution)/shard_map/gemm_units/pallas_call | solution.py:331
  304.5 3.5 collective-permute-start.13
  308.0 10.4 %contract_windows.1 = f32[6,2,128,128]{3,2,1,0:T(8,128)S(1)} custom-call(s32[475]{0:T(512)S(1)} %get-tuple-element.237, s32[2]{0:T(128)S(1)} %get-tuple-element.253, f32[4,1536,256]{2,1,0:T(8,128)} %gemm_units.10.mine, f32[2,24,2,128,128]{4,3,2,1,0:T(8,128)} %find_windows.1.near, f32[2,24,2,128,128]{4,3,2,1,0:T(8,128)} %collective-permute-done.14.far), custom_call_target="tpu_custom_call" | custom-call | tf_op jit(solution)/shard_map/contract_windows/pallas_call | solution.py:465
  321.0 6.6 %finish_columns.2.refs_0_ = f32[4,2,1536,128]{3,2,1,0:T(8,128)} custom-call(s32[475]{0:T(512)S(1)} %get-tuple-element.237, s32[4]{0:T(128)S(1)} %copy-done.3, f32[4,1536,256]{2,1,0:T(8,128)} %gemm_units.10.mine, f32[4,1536,256]{2,1,0:T(8,128)} %collective-permute-done.13.other, f32[2,2,128,128]{3,2,1,0:T(8,128)S(1)} %copy-done.1), custom_call_target="tpu_custom_call" | custom-call | flops 603979776 | bytes 9437184 | tf_op jit(solution)/shard_map/finish_columns/pallas_call | solution.py:530
  327.8 3.4 collective-permute-start.18
  331.6 6.6 %finish_columns.3 = f32[4,2,1536,128]{3,2,1,0:T(8,128)} custom-call(s32[475]{0:T(512)S(1)} %get-tuple-element.237, s32[4]{0:T(128)S(1)} %copy-done.3, f32[4,1536,256]{2,1,0:T(8,128)} %gemm_units.10.mine, f32[4,1536,256]{2,1,0:T(8,128)} %collective-permute-done.13.other, f32[2,2,128,128]{3,2,1,0:T(8,128)S(1)} %copy-done.1, ...), custom_call_target="tpu_custom_call", output_to_operand_aliasing={{}: (5, {})} | custom-call | flops 603979776 | bytes 9437184 | tf_op jit(solution)/shard_map/finish_columns/pallas_call | solution.py:530
  347.1 4.4 %collective-permute-done.23 = f32[4,96,128]{2,1,0:T(8,128)S(1)} collective-permute-done((f32[4,96,128]{2,1,0:T(8,128)S(1)}, f32[4,96,128]{2,1,0:T(8,128)S(1)}, u32[]{:S(2)}, u32[]{:S(2)}) %collective-permute-start.23) | collective-permute-done | bytes 196640 | tf_op jit(solution)/shard_map/ppermute | solution.py:598
  354.4 3.0 finish_diagonals.1
  (68 shorter events, 36.9 us)
Async XLA Ops:
  16.7 61.0 %collective-permute-start = (f32[20,2,128,128]{3,2,1,0:T(8,128)S(1)}, f32[20,2,128,128]{3,2,1,0:T(8,128)}, u32[]{:S(2)}, u32[]{:S(2)}) collective-permute-start(f32[20,2,128,128]{3,2,1,0:T(8,128)S(1)} %get-tuple-element.80.refs_1_.refs_0_), channel_id=1, source_target_pairs={{0,4},{2,6},{4,8},{6,10},{8,12},{10,14},{1,5},{3,7},{5,9},{7,11},{... | collective-permute-start | bytes 7864328 | tf_op jit(solution)/shard_map/ppermute | solution.py:594
  23.2 60.3 %collective-permute-start.1 = (f32[20,2,128,128]{3,2,1,0:T(8,128)S(1)}, f32[20,2,128,128]{3,2,1,0:T(8,128)}, u32[]{:S(2)}, u32[]{:S(2)}) collective-permute-start(f32[20,2,128,128]{3,2,1,0:T(8,128)S(1)} %get-tuple-element.80.refs_1_.refs_0_), channel_id=1, source_target_pairs={{4,0},{6,2},{8,4},{10,6},{12,8},{14,10},{5,1},{7,3},{9,5},{11,7},{... | collective-permute-start | bytes 7864328 | tf_op jit(solution)/shard_map/ppermute | solution.py:594
  24.5 59.0 %collective-permute-start.2 = (f32[20,2,128,128]{3,2,1,0:T(8,128)S(1)}, f32[20,2,128,128]{3,2,1,0:T(8,128)}, u32[]{:S(2)}, u32[]{:S(2)}) collective-permute-start(f32[20,2,128,128]{3,2,1,0:T(8,128)S(1)} %get-tuple-element.80.refs_1_.refs_0_), channel_id=1, source_target_pairs={{0,2},{2,0},{4,6},{6,4},{8,10},{10,8},{12,14},{14,12},{1,3},{3,1},... | collective-permute-start | bytes 7864328 | tf_op jit(solution)/shard_map/ppermute | solution.py:598
  83.5 64.9 %collective-permute-start.3 = (f32[20,2,128,128]{3,2,1,0:T(8,128)}, f32[20,2,128,128]{3,2,1,0:T(8,128)}, u32[]{:S(2)}, u32[]{:S(2)}) collective-permute-start(f32[20,2,128,128]{3,2,1,0:T(8,128)} %collective-permute-done.refs_2_.refs_1_), channel_id=1, source_target_pairs={{4,8},{6,10},{8,12},{10,14},{5,9},{7,11},{9,13},{11,15},{20,24},{2... | collective-permute-start | bytes 7864328 | tf_op jit(solution)/shard_map/ppermute | solution.py:594
  85.7 62.8 %collective-permute-start.4 = (f32[20,2,128,128]{3,2,1,0:T(8,128)}, f32[20,2,128,128]{3,2,1,0:T(8,128)}, u32[]{:S(2)}, u32[]{:S(2)}) collective-permute-start(f32[20,2,128,128]{3,2,1,0:T(8,128)} %collective-permute-done.1.refs_3_.refs_2_), channel_id=1, source_target_pairs={{4,0},{6,2},{8,4},{10,6},{5,1},{7,3},{9,5},{11,7},{20,16},{22,18},... | collective-permute-start | bytes 7864328 | tf_op jit(solution)/shard_map/ppermute | solution.py:594
  90.7 57.7 %collective-permute-start.6 = (f32[20,2,128,128]{3,2,1,0:T(8,128)}, f32[20,2,128,128]{3,2,1,0:T(8,128)}, u32[]{:S(2)}, u32[]{:S(2)}) collective-permute-start(f32[20,2,128,128]{3,2,1,0:T(8,128)} %broadcast_select_fusion.1), channel_id=1, source_target_pairs={{0,2},{2,0},{4,6},{6,4},{8,10},{10,8},{12,14},{14,12},{1,3},{3,1},... | collective-permute-start | bytes 7864328 | tf_op jit(solution)/shard_map/ppermute | solution.py:598
  92.2 60.0 %collective-permute-start.5 = (f32[20,2,128,128]{3,2,1,0:T(8,128)}, f32[20,2,128,128]{3,2,1,0:T(8,128)}, u32[]{:S(2)}, u32[]{:S(2)}) collective-permute-start(f32[20,2,128,128]{3,2,1,0:T(8,128)} %collective-permute-done.2.refs_4_.refs_3_), channel_id=1, source_target_pairs={{0,4},{2,6},{12,8},{14,10},{1,5},{3,7},{13,9},{15,11},{16,20},{18,... | collective-permute-start | bytes 7864328 | tf_op jit(solution)/shard_map/ppermute | solution.py:671
  152.3 61.1 %collective-permute-start.7 = (f32[20,2,128,128]{3,2,1,0:T(8,128)}, f32[20,2,128,128]{3,2,1,0:T(8,128)S(1)}, u32[]{:S(2)}, u32[]{:S(2)}) collective-permute-start(f32[20,2,128,128]{3,2,1,0:T(8,128)} %collective-permute-done.3.refs_2_.refs_4_), channel_id=1, source_target_pairs={{8,12},{10,14},{9,13},{11,15},{24,28},{26,30},{25,29},{27,31}} | collective-permute-start | bytes 7864328 | tf_op jit(solution)/shard_map/ppermute | solution.py:594
  155.3 71.4 %collective-permute-start.8 = (f32[20,2,128,128]{3,2,1,0:T(8,128)}, f32[20,2,128,128]{3,2,1,0:T(8,128)S(1)}, u32[]{:S(2)}, u32[]{:S(2)}) collective-permute-start(f32[20,2,128,128]{3,2,1,0:T(8,128)} %collective-permute-done.4.refs_3_.refs_5_), channel_id=1, source_target_pairs={{4,0},{6,2},{5,1},{7,3},{20,16},{22,18},{21,17},{23,19}} | collective-permute-start | bytes 7864328 | tf_op jit(solution)/shard_map/ppermute | solution.py:594
  156.6 56.7 %collective-permute-start.9 = (f32[20,2,128,128]{3,2,1,0:T(8,128)S(1)}, f32[20,2,128,128]{3,2,1,0:T(8,128)S(1)}, u32[]{:S(2)}, u32[]{:S(2)}) collective-permute-start(f32[20,2,128,128]{3,2,1,0:T(8,128)S(1)} %broadcast_select_fusion), channel_id=1, source_target_pairs={{0,2},{2,0},{4,6},{6,4},{8,10},{10,8},{12,14},{14,12},{1,3},{3,1},... | collective-permute-start | bytes 7864328 | tf_op jit(solution)/shard_map/ppermute | solution.py:598
  226.9 56.9 %collective-permute-start.10 = (f32[10,2,128,128]{3,2,1,0:T(8,128)S(1)}, f32[10,2,128,128]{3,2,1,0:T(8,128)S(1)}, u32[]{:S(2)}, u32[]{:S(2)}) collective-permute-start(f32[10,2,128,128]{3,2,1,0:T(8,128)S(1)} %slice.10), channel_id=1, source_target_pairs={{8,12},{10,14},{9,13},{11,15},{24,28},{26,30},{25,29},{27,31}} | collective-permute-start | bytes 3932168 | tf_op jit(solution)/shard_map/ppermute | solution.py:594
  227.6 56.2 %collective-permute-start.11 = (f32[10,2,128,128]{3,2,1,0:T(8,128)S(1)}, f32[10,2,128,128]{3,2,1,0:T(8,128)S(1)}, u32[]{:S(2)}, u32[]{:S(2)}) collective-permute-start(f32[10,2,128,128]{3,2,1,0:T(8,128)S(1)} %slice.10), channel_id=1, source_target_pairs={{4,0},{6,2},{5,1},{7,3},{20,16},{22,18},{21,17},{23,19}} | collective-permute-start | bytes 3932168 | tf_op jit(solution)/shard_map/ppermute | solution.py:594
  230.2 53.5 %collective-permute-start.12 = (f32[10,2,128,128]{3,2,1,0:T(8,128)}, f32[10,2,128,128]{3,2,1,0:T(8,128)S(1)}, u32[]{:S(2)}, u32[]{:S(2)}) collective-permute-start(f32[10,2,128,128]{3,2,1,0:T(8,128)} %slice_select_fusion), channel_id=1, source_target_pairs={{0,2},{2,0},{4,6},{6,4},{8,10},{10,8},{12,14},{14,12},{1,3},{3,1},... | collective-permute-start | bytes 3932168 | tf_op jit(solution)/shard_map/ppermute | solution.py:598
  283.7 24.3 %collective-permute-start.14 = (f32[2,24,2,128,128]{4,3,2,1,0:T(8,128)}, f32[2,24,2,128,128]{4,3,2,1,0:T(8,128)}, u32[]{:S(2)}, u32[]{:S(2)}) collective-permute-start(f32[2,24,2,128,128]{4,3,2,1,0:T(8,128)} %find_windows.1.near), channel_id=1, source_target_pairs={{0,1},{1,0},{2,3},{3,2},{4,5},{5,4},{6,7},{7,6},{8,9},{9,8},{10,11... | collective-permute-start | bytes 18874376 | tf_op jit(solution)/shard_map/ppermute | solution.py:598
  304.5 14.0 %collective-permute-start.13 = (f32[4,1536,256]{2,1,0:T(8,128)}, f32[4,1536,256]{2,1,0:T(8,128)}, u32[]{:S(2)}, u32[]{:S(2)}) collective-permute-start(f32[4,1536,256]{2,1,0:T(8,128)} %gemm_units.10.mine), channel_id=1, source_target_pairs={{0,1},{1,0},{2,3},{3,2},{4,5},{5,4},{6,7},{7,6},{8,9},{9,8},{10,11... | collective-permute-start | bytes 18874376 | tf_op jit(solution)/shard_map/ppermute | solution.py:598
  318.5 1.8 collective-permute-start.15
  320.4 7.3 %collective-permute-start.16 = (f32[4,96,128]{2,1,0:T(8,128)S(1)}, f32[4,96,128]{2,1,0:T(8,128)S(1)}, u32[]{:S(2)}, u32[]{:S(2)}) collective-permute-start(f32[4,96,128]{2,1,0:T(8,128)S(1)} %dynamic-slice_bitcast_fusion.1), channel_id=1, source_target_pairs={{0,2},{2,0},{4,6},{6,4},{8,10},{10,8},{12,14},{14,12},{1,3},{3,1},... | collective-permute-start | bytes 589832 | tf_op jit(solution)/shard_map/ppermute | solution.py:598
  327.7 10.5 %collective-permute-start.17 = (f32[96,128]{1,0:T(8,128)S(1)}, f32[96,128]{1,0:T(8,128)S(1)}, u32[]{:S(2)}, u32[]{:S(2)}) collective-permute-start(f32[96,128]{1,0:T(8,128)S(1)} %get-tuple-element.140), channel_id=1, source_target_pairs={{0,4},{2,6},{4,8},{6,10},{8,12},{10,14},{12,0},{14,2},{1,5},{3,7},... | collective-permute-start | bytes 147464 | tf_op jit(solution)/shard_map/ppermute | solution.py:618
  327.8 10.4 %collective-permute-start.18 = (f32[96,128]{1,0:T(8,128)S(1)}, f32[96,128]{1,0:T(8,128)S(1)}, u32[]{:S(2)}, u32[]{:S(2)}) collective-permute-start(f32[96,128]{1,0:T(8,128)S(1)} %get-tuple-element.139), channel_id=1, source_target_pairs={{0,8},{2,10},{4,12},{6,14},{8,0},{10,2},{12,4},{14,6},{1,9},{3,11}... | collective-permute-start | bytes 147464 | tf_op jit(solution)/shard_map/ppermute | solution.py:618
  331.2 7.0 %collective-permute-start.19 = (f32[96,128]{1,0:T(8,128)S(1)}, f32[96,128]{1,0:T(8,128)S(1)}, u32[]{:S(2)}, u32[]{:S(2)}) collective-permute-start(f32[96,128]{1,0:T(8,128)S(1)} %get-tuple-element.138), channel_id=1, source_target_pairs={{0,12},{2,14},{4,0},{6,2},{8,4},{10,6},{12,8},{14,10},{1,13},{3,15... | collective-permute-start | bytes 147464 | tf_op jit(solution)/shard_map/ppermute | solution.py:618
  338.3 6.5 %collective-permute-start.20 = (f32[96,128]{1,0:T(8,128)S(1)}, f32[96,128]{1,0:T(8,128)S(1)}, u32[]{:S(2)}, u32[]{:S(2)}) collective-permute-start(f32[96,128]{1,0:T(8,128)S(1)} %get-tuple-element.133), channel_id=1, source_target_pairs={{0,4},{2,6},{4,8},{6,10},{8,12},{10,14},{12,0},{14,2},{1,5},{3,7},... | collective-permute-start | bytes 147464 | tf_op jit(solution)/shard_map/ppermute | solution.py:618
  340.0 5.8 %collective-permute-start.21 = (f32[96,128]{1,0:T(8,128)S(1)}, f32[96,128]{1,0:T(8,128)S(1)}, u32[]{:S(2)}, u32[]{:S(2)}) collective-permute-start(f32[96,128]{1,0:T(8,128)S(1)} %get-tuple-element.133), channel_id=1, source_target_pairs={{0,8},{2,10},{4,12},{6,14},{8,0},{10,2},{12,4},{14,6},{1,9},{3,11}... | collective-permute-start | bytes 147464 | tf_op jit(solution)/shard_map/ppermute | solution.py:618
  340.5 5.2 %collective-permute-start.22 = (f32[96,128]{1,0:T(8,128)S(1)}, f32[96,128]{1,0:T(8,128)S(1)}, u32[]{:S(2)}, u32[]{:S(2)}) collective-permute-start(f32[96,128]{1,0:T(8,128)S(1)} %get-tuple-element.133), channel_id=1, source_target_pairs={{0,12},{2,14},{4,0},{6,2},{8,4},{10,6},{12,8},{14,10},{1,13},{3,15... | collective-permute-start | bytes 147464 | tf_op jit(solution)/shard_map/ppermute | solution.py:618
  345.8 5.7 %collective-permute-start.23 = (f32[4,96,128]{2,1,0:T(8,128)S(1)}, f32[4,96,128]{2,1,0:T(8,128)S(1)}, u32[]{:S(2)}, u32[]{:S(2)}) collective-permute-start(f32[4,96,128]{2,1,0:T(8,128)S(1)} %bitcast_dynamic-update-slice_fusion), channel_id=1, source_target_pairs={{0,2},{2,0},{4,6},{6,4},{8,10},{10,8},{12,14},{14,12},{1,3},{3,1},... | collective-permute-start | bytes 589832 | tf_op jit(solution)/shard_map/ppermute | solution.py:598
  (5 other events, 20.0 us)
